TPU v7x, 32 devices: a whole 2x2x4 slice. The times are simulated.
32 devices in a mesh: groups: 2 (over y), seq: 4 (over z), exp: 4 (over x, core).
Axes of the slice: x: 2, y: 2, z: 4, core: 2. Of those that a mesh axis runs over, the one named last changes fastest.
Arguments:
- residual: bfloat16 [1024, 6144], P(('groups', 'seq'), 'exp'), parts along dimension 0, may hold values from -6 to 6
- query_rows: bfloat16 [1024, 6144], P(('groups', 'seq'), 'exp'), parts along dimension 0, may hold values from -6 to 6
- key_rows: bfloat16 [1024, 6144], P(('groups', 'seq'), 'exp'), parts along dimension 0, may hold values from -6 to 6
- value_rows: bfloat16 [1024, 6144], P(('groups', 'seq'), 'exp'), parts along dimension 0, may hold values from -6 to 6
- log_decay: float32 [1024, 48], P(('groups', 'seq'), 'exp'), parts along dimension 0, may hold values from -0.8 to 0
- attn_gain: float32 [6144], P('exp'), may hold values from 0.1 to 1.9
- norm_gain: float32 [6144], P('exp'), may hold values from 0.1 to 1.9
- router: bfloat16 [6144, 32], P('exp'), may hold values from -0.3125 to 0.3125
- expert_ids: int32 [1024, 2], P(('groups', 'seq')), parts along dimension 0, may hold values from 0 to 31, all different within a row
- priority: int32 [8, 128], P(('groups', 'seq')), parts along dimension 0, may hold values from 0 to 127, each once within a row
- gate_weight: bfloat16 [4, 6144, 4608], P('exp', None, 'seq'), may hold values from -0.078125 to 0.078125
- up_weight: bfloat16 [4, 6144, 4608], P('exp', None, 'seq'), may hold values from -0.078125 to 0.078125
- down_weight: bfloat16 [4, 4608, 6144], P('exp', None, 'seq'), may hold values from -0.125 to 0.125
Outputs:
- layer_out: bfloat16 [1024, 6144], P(('groups', 'seq'), 'exp'), parts along dimension 0
There are 2 independent parts, one for each index of `groups`. A program takes and returns all parts, laid end to end along the dimension named above; an argument that names none is the same for every part. Nothing has to cross between parts.
Inputs may be any that keep to these rules, and one draw needn't show every extreme that they name: `expert_ids`: each row names two different experts; ids of 4 or more name experts whose weights are not given. `priority`: each row holds every number from 0 to 127 once.
All inputs are finite; a program needn't handle non-finite values.
Results may differ from a plain program's by a relative error of at most 0.0047.
Values may be sent and summed in bfloat16 or wider, within the bound.
A program may use at most 128 MiB of HBM per device.

v0:
```python
import jax
import jax.numpy as jnp
from jax import lax
from jax.sharding import PartitionSpec as P

D = 6144
HEAD = 128
EXPERTS = 32
CAP = 8


def link_states(earlier, later):
    return (earlier[0] * later[0], later[0] * earlier[1] + later[1])


def body(
    residual,
    query_rows,
    key_rows,
    value_rows,
    log_decay,
    attn_gain,
    norm_gain,
    router,
    expert_ids,
    priority,
    gate_weight,
    up_weight,
    down_weight,
):
    rows = residual.shape[0]
    width = residual.shape[1]
    heads = width // HEAD
    held = lax.axis_size("exp")
    queries = query_rows.reshape(rows, heads, HEAD)
    keys_local = key_rows.reshape(rows, heads, HEAD)
    values = value_rows.reshape(rows, heads, HEAD)
    cumulative = jnp.cumsum(log_decay, axis=0)
    scores = jnp.einsum("thd,shd->hts", queries, keys_local, preferred_element_type=jnp.float32)
    causal = (jnp.arange(rows)[:, None] >= jnp.arange(rows)[None, :])[None]
    spread = cumulative.T[:, :, None] - cumulative.T[:, None, :]
    weights = jnp.where(causal, scores * jnp.exp(jnp.where(causal, spread, 0.0)), 0.0).astype(
        jnp.bfloat16
    )
    local_part = jnp.einsum("hts,shd->thd", weights, values, preferred_element_type=jnp.float32)
    to_end = jnp.exp(cumulative[-1][None, :] - cumulative)
    keyed = (keys_local.astype(jnp.float32) * to_end[:, :, None]).astype(jnp.bfloat16)
    block_state = jnp.einsum("thd,the->hde", keyed, values, preferred_element_type=jnp.float32)
    block_decay = jnp.exp(cumulative[-1])
    seq_count = lax.axis_size("seq")
    share_size = block_state.size // seq_count
    flat_state = block_state.reshape(seq_count, share_size)
    tiled_decay = jnp.broadcast_to(block_decay[None, :], (seq_count, heads))
    arrived_state, arrived_decay = (
        lax.all_to_all(flat_state, "seq", split_axis=0, concat_axis=0, tiled=True),
        lax.all_to_all(tiled_decay, "seq", split_axis=0, concat_axis=0, tiled=True),
    )
    position = lax.axis_index("seq") * share_size + jnp.arange(share_size, dtype=jnp.int32)
    owner_head = position // (HEAD * HEAD)
    selector = jnp.where(
        owner_head[None, :] == jnp.arange(heads, dtype=jnp.int32)[:, None], 1.0, 0.0
    ).astype(jnp.float32)
    element_decay = jnp.dot(arrived_decay, selector, precision=lax.Precision.HIGHEST)
    inclusive = lax.associative_scan(link_states, (element_decay, arrived_state), axis=0)[1]
    exclusive = jnp.concatenate([jnp.zeros((1, share_size), jnp.float32), inclusive[:-1]], axis=0)
    returned_prefix = lax.all_to_all(exclusive, "seq", split_axis=0, concat_axis=0, tiled=True)
    prior_state = returned_prefix.reshape(block_state.shape)
    inter = jnp.einsum(
        "thd,hde->the", queries.astype(jnp.float32), prior_state, precision=lax.Precision.HIGHEST
    )
    attended = local_part + jnp.exp(cumulative)[:, :, None] * inter
    normed = attended * lax.rsqrt(jnp.mean(attended * attended, axis=-1, keepdims=True) + 1e-06)
    normed = normed * attn_gain.reshape(heads, HEAD)
    mixed = (residual.astype(jnp.float32) + normed.reshape(rows, width)).astype(jnp.bfloat16)
    mixed_f = mixed.astype(jnp.float32)
    gained = mixed_f * norm_gain
    router_f = router.astype(jnp.float32)
    squares = lax.psum(jnp.sum(mixed_f * mixed_f, axis=1), "exp")
    inverse = lax.rsqrt(squares / D + 1e-06)
    scaled = gained * inverse[:, None]
    logits = lax.psum(jnp.dot(scaled, router_f, precision=lax.Precision.HIGHEST), "exp")
    tokens_in = scaled.astype(jnp.bfloat16)
    probs = jax.nn.sigmoid(logits)
    chosen = expert_ids[:, :, None] == jnp.arange(EXPERTS, dtype=jnp.int32)[None, None, :]
    selected = jnp.sum(jnp.where(chosen, probs[:, None, :], 0.0), axis=-1)
    gates = selected / jnp.sum(selected, axis=-1, keepdims=True)
    is_held = expert_ids[:, :, None] == jnp.arange(held, dtype=jnp.int32)[None, None, :]
    member = jnp.where(jnp.any(is_held, axis=1), 1.0, 0.0).astype(jnp.float32)
    gate_held = jnp.sum(jnp.where(is_held, gates[:, :, None], 0.0), axis=1)
    order = priority[0]
    earlier = jnp.where(order[None, :] < order[:, None], 1.0, 0.0).astype(jnp.bfloat16)
    rank = jnp.dot(earlier, member.astype(jnp.bfloat16), preferred_element_type=jnp.float32)
    kept = (member > 0.5) & (rank < CAP)
    slot_ids = jnp.arange(CAP).astype(jnp.float32)
    place = kept.T[:, None, :] & (rank.T[:, None, :] == slot_ids[None, :, None])
    place_f = jnp.where(place, 1.0, 0.0).astype(jnp.float32)
    buffer = jnp.einsum(
        "ect,td->ecd", place_f.astype(jnp.bfloat16), tokens_in, preferred_element_type=jnp.float32
    ).astype(jnp.bfloat16)
    arrived = lax.all_to_all(buffer, "exp", split_axis=0, concat_axis=2, tiled=True)[0]
    gathered = lax.all_gather(arrived, "seq", axis=0, tiled=True)
    gate = jnp.dot(gathered, gate_weight[0], preferred_element_type=jnp.float32)
    up = jnp.dot(gathered, up_weight[0], preferred_element_type=jnp.float32)
    hidden = (jax.nn.silu(gate) * up).astype(jnp.bfloat16)
    weight_rows = down_weight[0]
    summed = jnp.dot(
        lax.all_gather(hidden, "seq", axis=1, tiled=True),
        weight_rows,
        preferred_element_type=jnp.float32,
    )
    expert_out = summed.astype(jnp.bfloat16)
    returned = lax.all_to_all(expert_out, "seq", split_axis=0, concat_axis=1, tiled=True)
    regrouped = lax.all_to_all(returned[None], "exp", split_axis=2, concat_axis=0, tiled=True)
    weighted = place_f * gate_held.T[:, None, :]
    combined = jnp.einsum(
        "ect,ecd->td", weighted, regrouped.astype(jnp.float32), precision=lax.Precision.HIGHEST
    )
    return (mixed_f + combined).astype(jnp.bfloat16)


def solution(mesh):
    return jax.shard_map(
        body,
        mesh=mesh,
        in_specs=(
            P(("groups", "seq"), "exp"),
            P(("groups", "seq"), "exp"),
            P(("groups", "seq"), "exp"),
            P(("groups", "seq"), "exp"),
            P(("groups", "seq"), "exp"),
            P("exp"),
            P("exp"),
            P("exp", None),
            P(("groups", "seq"), None),
            P(("groups", "seq"), None),
            P("exp", None, "seq"),
            P("exp", None, "seq"),
            P("exp", None, "seq"),
        ),
        out_specs=P(("groups", "seq"), "exp"),
        check_vma=False,
    )
```

profile of v0, /device:TPU:3, one launch (start us, length us, event | category | flops | bytes accessed | tf_op | source)
XLA Modules:
  0.0 214.6 jit_solution(99139282639434964)
XLA Ops:
  0.0 0.8 copy.111
  1.0 0.6 broadcast_in_dim.109
  1.6 4.6 %all-to-all-start.1 = ((f32[4,1,12]{2,1,0:T(1,128)}), f32[4,1,12]{2,1,0:T(1,128)S(1)}, u32[]{:S(2)}, u32[]{:S(2)}) async-start(f32[4,1,12]{2,1,0:T(1,128)} %broadcast_in_dim.109), calls=%async_computation.1 | async-start | bytes 4096 | tf_op jit(solution)/shard_map/all_to_all | solution.py:56
  6.2 1.2 copy.114
  7.4 1.2 copy.108
  8.7 1.3 fusion.37
  10.0 0.5 all-to-all-done.1
  10.5 4.1 %all-to-all-start = ((f32[4,1,49152]{2,1,0:T(1,128)}), f32[4,1,49152]{2,1,0:T(1,128)S(1)}, u32[]{:S(2)}, u32[]{:S(2)}) async-start(f32[4,1,49152]{2,1,0:T(1,128)} %bitcast.6), calls=%async_computation | async-start | bytes 1572864 | tf_op jit(solution)/shard_map/all_to_all | solution.py:55
  14.7 1.9 fusion.6
  16.6 2.8 %slice.56 = f32[2,49152]{1,0:T(2,128)S(1)} slice(f32[4,49152]{1,0:T(4,128)S(1)} %fusion.6), slice={[1:4:2], [0:49152:1]} | slice | bytes 786432 | tf_op jit(solution)/shard_map/slice | solution.py:64
  19.5 5.1 %slice.60 = f32[2,49152]{1,0:T(2,128)} slice(f32[4,49152]{1,0:T(4,128)S(1)} %fusion.6), slice={[0:3:2], [0:49152:1]} | slice | bytes 786432 | tf_op jit(solution)/shard_map/slice | solution.py:64
  24.6 9.6 %all-to-all-done = f32[4,1,49152]{2,1,0:T(1,128)S(1)} async-done(((f32[4,1,49152]{2,1,0:T(1,128)}), f32[4,1,49152]{2,1,0:T(1,128)S(1)}, u32[]{:S(2)}, u32[]{:S(2)}) %all-to-all-start) | async-done | bytes 786464 | tf_op jit(solution)/shard_map/all_to_all | solution.py:55
  34.2 0.5 copy.133
  34.7 2.8 %slice.58 = f32[2,49152]{1,0:T(2,128)S(1)} slice(f32[4,49152]{1,0:T(4,128)S(1)} %bitcast.98), slice={[1:4:2], [0:49152:1]} | slice | bytes 786432 | tf_op jit(solution)/shard_map/slice | solution.py:64
  37.5 5.1 %slice.57 = f32[2,49152]{1,0:T(2,128)} slice(f32[4,49152]{1,0:T(4,128)S(1)} %bitcast.99), slice={[0:3:2], [0:49152:1]} | slice | bytes 786432 | tf_op jit(solution)/shard_map/slice | solution.py:64
  42.7 1.3 multiply_add_fusion
  43.9 1.6 fusion.86
  45.9 1.7 fusion.52
  47.6 0.4 pad_maximum_fusion
  47.9 0.6 pad.21
  48.5 0.6 pad.39
  49.6 1.7 copy.119
  51.3 3.5 %all-to-all-start.2 = ((f32[4,1,49152]{2,1,0:T(1,128)}), f32[4,1,49152]{2,1,0:T(1,128)S(1)}, u32[]{:S(2)}, u32[]{:S(2)}) async-start(f32[4,1,49152]{2,1,0:T(1,128)} %copy.119), calls=%async_computation.2 | async-start | bytes 1572864 | tf_op jit(solution)/shard_map/all_to_all | solution.py:66
  54.8 1.2 copy.107
  56.4 17.9 %all-to-all-done.2 = f32[4,1,49152]{2,1,0:T(1,128)S(1)} async-done(((f32[4,1,49152]{2,1,0:T(1,128)}), f32[4,1,49152]{2,1,0:T(1,128)S(1)}, u32[]{:S(2)}, u32[]{:S(2)}) %all-to-all-start.2) | async-done | bytes 786464 | tf_op jit(solution)/shard_map/all_to_all | solution.py:66
  74.4 0.8 fusion.27
  75.2 0.7 multiply_reduce_fusion
  76.6 6.5 %psum.14 = f32[128]{0:T(128)S(1)} all-reduce(f32[128]{0:T(128)S(1)} %get-tuple-element.7), channel_id=1, replica_groups=mesh['groups'=2,'seq'=4,'exp'=4] {'exp'}, use_global_device_ids=true, to_apply=%region_4.5 | all-reduce | flops 128 | bytes 1024 | tf_op jit(solution)/shard_map/psum | solution.py:78
  83.1 0.9 convolution_convert_fusion
  84.0 4.4 %all-to-all-start.3 = ((bf16[4,8,1536]{2,1,0:T(8,128)(2,1)}), bf16[4,8,1536]{2,1,0:T(8,128)(2,1)S(1)}, u32[]{:S(2)}, u32[]{:S(2)}) async-start(bf16[4,8,1536]{2,1,0:T(8,128)(2,1)} %convolution_convert_fusion), calls=%async_computation.3 | async-start | bytes 196608 | tf_op jit(solution)/shard_map/all_to_all | solution.py:100
  88.4 0.7 fusion.31
  89.1 9.5 %psum.15 = f32[128,32]{0,1:T(8,128)S(1)} all-reduce(f32[128,32]{0,1:T(8,128)S(1)} %fusion.31), channel_id=1, replica_groups=mesh['groups'=2,'seq'=4,'exp'=4] {'exp'}, use_global_device_ids=true, to_apply=%region_5.6 | all-reduce | flops 4096 | bytes 32768 | tf_op jit(solution)/shard_map/psum | solution.py:81
  98.6 11.6 %all_gather.6 = bf16[32,6144]{1,0:T(8,128)(2,1)S(1)} all-gather(bf16[8,6144]{1,0:T(8,128)(2,1)S(1)} %bitcast.110), channel_id=1, replica_groups=mesh['groups'=2,'seq'=4,'exp'=4] {'seq'}, dimensions={0}, use_global_device_ids=true | all-gather | bytes 491520 | tf_op jit(solution)/shard_map/all_gather | solution.py:101
  110.2 7.6 %fusion.4 = f32[32,1152]{1,0:T(8,128)S(1)} fusion(bf16[32,6144]{1,0:T(8,128)(2,1)S(1)} %all_gather.6, bf16[1,6144,1152]{2,1,0:T(8,128)(2,1)} %param.23), kind=kOutput, calls=%fused_computation.4 | convolution fusion | flops 452984832 | bytes 14696448 | tf_op jit(solution)/shard_map/dot_general | solution.py:102
  117.8 7.6 %fusion.13 = bf16[32,1152]{1,0:T(8,128)(2,1)S(1)} fusion(bf16[32,6144]{1,0:T(8,128)(2,1)S(1)} %all_gather.6, bf16[1,6144,1152]{2,1,0:T(8,128)(2,1)} %param.24, f32[32,1152]{1,0:T(8,128)S(1)} %fusion.4), kind=kOutput, calls=%fused_computation.13 | convolution fusion | flops 453206016 | bytes 14770176 | tf_op jit(solution)/shard_map/dot_general | solution.py:103
  125.4 11.5 %all_gather.7 = bf16[32,4608]{1,0:T(8,128)(2,1)S(1)} all-gather(bf16[32,1152]{1,0:T(8,128)(2,1)S(1)} %fusion.13), channel_id=1, replica_groups=mesh['groups'=2,'seq'=4,'exp'=4] {'seq'}, dimensions={1}, use_global_device_ids=true | all-gather | bytes 368640 | tf_op jit(solution)/shard_map/all_gather | solution.py:107
  136.9 3.2 %fusion.19 = bf16[4,8,1536]{2,1,0:T(8,128)(2,1)} fusion(bf16[32,4608]{1,0:T(8,128)(2,1)S(1)} %all_gather.7, bf16[1,4608,1536]{2,1,0:T(8,128)(2,1)S(1)} %bitcast.94), kind=kOutput, calls=%fused_computation.16 | convolution fusion | flops 453033984 | bytes 14548992 | tf_op jit(solution)/shard_map/dot_general | solution.py:106
  140.0 3.3 %all-to-all-start.4 = ((bf16[4,8,1536]{2,1,0:T(8,128)(2,1)}), bf16[4,8,1536]{2,1,0:T(8,128)(2,1)S(1)}, u32[]{:S(2)}, u32[]{:S(2)}) async-start(bf16[4,8,1536]{2,1,0:T(8,128)(2,1)} %fusion.19), calls=%async_computation.4 | async-start | bytes 196608 | tf_op jit(solution)/shard_map/all_to_all | solution.py:112
  143.4 4.7 %all-to-all-done.4 = bf16[4,8,1536]{2,1,0:T(8,128)(2,1)S(1)} async-done(((bf16[4,8,1536]{2,1,0:T(8,128)(2,1)}), bf16[4,8,1536]{2,1,0:T(8,128)(2,1)S(1)}, u32[]{:S(2)}, u32[]{:S(2)}) %all-to-all-start.4) | async-done | bytes 98336 | tf_op jit(solution)/shard_map/all_to_all | solution.py:112
  148.1 3.9 %copy.123 = bf16[1,8,6144]{1,0,2:T(2,128)(2,1)S(1)} copy(bf16[1,8,6144]{2,1,0:T(8,128)(2,1)S(1)} %bitcast.108) | data formatting | bytes 196608 | tf_op jit(solution)/shard_map/broadcast_in_dim | solution.py:113
  152.0 0.6 broadcast.113
  152.6 34.4 %reduce.1 = bf16[6144,8]{1,0:T(8,128)(2,1)} reduce(bf16[6144,1,8]{2,1,0:T(2,128)(2,1)S(1)} %bitcast.95, bf16[]{:T(256)} %broadcast.113), dimensions={1}, to_apply=%bitcast.78.reduce_sub_computation | reduce | bytes 196610
  187.0 3.7 %reshape.134 = bf16[4,2,6144]{2,1,0:T(2,128)(2,1)} reshape(bf16[6144,8]{1,0:T(8,128)(2,1)} %reduce.1) | data formatting | bytes 196608
  190.7 12.7 %all-to-all-start.5 = ((bf16[4,2,6144]{2,1,0:T(2,128)(2,1)}), bf16[4,2,6144]{2,1,0:T(2,128)(2,1)S(1)}, u32[]{:S(2)}, u32[]{:S(2)}) async-start(bf16[4,2,6144]{2,1,0:T(2,128)(2,1)} %reshape.134), calls=%async_computation.5 | async-start | bytes 196608 | tf_op jit(solution)/shard_map/all_to_all | solution.py:113
  203.4 2.4 %all-to-all-done.5 = bf16[4,2,6144]{2,1,0:T(2,128)(2,1)S(1)} async-done(((bf16[4,2,6144]{2,1,0:T(2,128)(2,1)}), bf16[4,2,6144]{2,1,0:T(2,128)(2,1)S(1)}, u32[]{:S(2)}, u32[]{:S(2)}) %all-to-all-start.5) | async-done | bytes 98336 | tf_op jit(solution)/shard_map/all_to_all | solution.py:113
  205.8 3.8 %reshape.135 = bf16[6144,1,8]{2,1,0:T(2,128)(2,1)S(1)} reshape(bf16[4,2,6144]{2,1,0:T(2,128)(2,1)S(1)} %all-to-all-done.5) | data formatting | bytes 196608
  209.6 2.7 %copy.124 = bf16[1,8,6144]{2,1,0:T(8,128)(2,1)S(1)} copy(bf16[1,8,6144]{1,0,2:T(2,128)(2,1)S(1)} %bitcast.96) | data formatting | bytes 196608 | tf_op jit(solution)/shard_map/all_to_all | solution.py:113
  212.3 2.4 %fusion.9 = bf16[128,1536]{1,0:T(8,128)(2,1)} fusion(bf16[4,8,1536]{2,1,0:T(8,128)(2,1)S(1)} %bitcast.109, bf16[128,1536]{1,0:T(8,128)(2,1)} %copy-done.2, f32[4,128]{1,0:T(4,128)S(1)} %bitcast.112, f32[4,128]{1,0:T(4,128)S(1)} %get-tuple-element.18, f32[8]{0:T(128)S(1)} %iota_convert_fusion, pred[4,128]{1,0:T(4,128)(4,1)S(1)} %get-tuple-element.17), kind=kOutput, calls=%fused_computation.11 | convolution fusion | flops 76103680 | bytes 889376 | tf_op jit(solution)/shard_map/ect,ecd->td/dot_general | solution.py:115
  (52 shorter events, 2.4 us)
Async XLA Ops:
  0.0 88.4 %copy-start = (bf16[1536,32]{0,1:T(8,128)(2,1)S(1)}, bf16[1536,32]{0,1:T(8,128)(2,1)}, u32[]{:S(2)}) copy-start(bf16[1536,32]{0,1:T(8,128)(2,1)} %param.20) | copy-start | bytes 294916
  1.0 55.2 %copy-start.6 = (s32[128,2]{0,1:T(2,128)S(1)}, s32[128,2]{0,1:T(2,128)}, u32[]{:S(2)}) copy-start(s32[128,2]{0,1:T(2,128)} %param.21) | copy-start | bytes 3076
  1.0 55.2 %copy-start.8 = (s32[1,128]{1,0:T(1,128)S(1)}, s32[1,128]{1,0:T(1,128)}, u32[]{:S(2)}) copy-start(s32[1,128]{1,0:T(1,128)} %param.22) | copy-start | bytes 1540
  1.6 8.9 %all-to-all-start.1 = ((f32[4,1,12]{2,1,0:T(1,128)}), f32[4,1,12]{2,1,0:T(1,128)S(1)}, u32[]{:S(2)}, u32[]{:S(2)}) async-start(f32[4,1,12]{2,1,0:T(1,128)} %broadcast_in_dim.109), calls=%async_computation.1 | async-start | bytes 4096 | tf_op jit(solution)/shard_map/all_to_all | solution.py:56
  10.5 23.7 %all-to-all-start = ((f32[4,1,49152]{2,1,0:T(1,128)}), f32[4,1,49152]{2,1,0:T(1,128)S(1)}, u32[]{:S(2)}, u32[]{:S(2)}) async-start(f32[4,1,49152]{2,1,0:T(1,128)} %bitcast.6), calls=%async_computation | async-start | bytes 1572864 | tf_op jit(solution)/shard_map/all_to_all | solution.py:55
  14.6 61.3 %copy-start.5 = (f32[1536]{0:T(1024)S(1)}, f32[1536]{0:T(1024)}, u32[]{:S(2)}) copy-start(f32[1536]{0:T(1024)} %param.18) | copy-start | bytes 18436
  16.6 8.0 %copy-start.3 = (f32[4,49152]{1,0:T(4,128)}, f32[4,49152]{1,0:T(4,128)S(1)}, u32[]{:S(2)}) copy-start(f32[4,49152]{1,0:T(4,128)S(1)} %fusion.6) | copy-start | bytes 2359300
  24.6 58.5 %copy-start.7 = (f32[1536]{0:T(1024)S(1)}, f32[1536]{0:T(1024)}, u32[]{:S(2)}) copy-start(f32[1536]{0:T(1024)} %param.19) | copy-start | bytes 18436
  43.9 32.5 %copy-start.4 = (bf16[128,1536]{1,0:T(8,128)(2,1)S(1)}, bf16[128,1536]{1,0:T(8,128)(2,1)}, u32[]{:S(2)}) copy-start(bf16[128,1536]{1,0:T(8,128)(2,1)} %param.13) | copy-start | bytes 1179652
  51.3 23.1 %all-to-all-start.2 = ((f32[4,1,49152]{2,1,0:T(1,128)}), f32[4,1,49152]{2,1,0:T(1,128)S(1)}, u32[]{:S(2)}, u32[]{:S(2)}) async-start(f32[4,1,49152]{2,1,0:T(1,128)} %copy.119), calls=%async_computation.2 | async-start | bytes 1572864 | tf_op jit(solution)/shard_map/all_to_all | solution.py:66
  76.6 48.7 %copy-start.2 = (bf16[128,1536]{1,0:T(8,128)(2,1)}, bf16[128,1536]{1,0:T(8,128)(2,1)S(1)}, u32[]{:S(2)}) copy-start(bf16[128,1536]{1,0:T(8,128)(2,1)S(1)} %get-tuple-element.8) | copy-start | bytes 1179652
  84.0 14.6 %all-to-all-start.3 = ((bf16[4,8,1536]{2,1,0:T(8,128)(2,1)}), bf16[4,8,1536]{2,1,0:T(8,128)(2,1)S(1)}, u32[]{:S(2)}, u32[]{:S(2)}) async-start(bf16[4,8,1536]{2,1,0:T(8,128)(2,1)} %convolution_convert_fusion), calls=%async_computation.3 | async-start | bytes 196608 | tf_op jit(solution)/shard_map/all_to_all | solution.py:100
  110.2 26.6 %slice-start = ((s8[14155776]{0:T(1024)(128)(4,1)}), s8[4194304]{0:T(1024)(128)(4,1)S(1)}, s32[]{:S(2)}) async-start(s8[14155776]{0:T(1024)(128)(4,1)} %bitcast.93), calls=%async_computation.6 | async-start | bytes 8388608
  110.2 26.6 %slice-start.1 = ((s8[14155776]{0:T(1024)(128)(4,1)}), s8[4194304]{0:T(1024)(128)(4,1)S(1)}, s32[]{:S(2)}) async-start(s8[14155776]{0:T(1024)(128)(4,1)} %bitcast.93), calls=%async_computation.7 | async-start | bytes 8388608
  117.8 19.1 %slice-start.2 = ((s8[14155776]{0:T(1024)(128)(4,1)}), s8[4194304]{0:T(1024)(128)(4,1)S(1)}, s32[]{:S(2)}) async-start(s8[14155776]{0:T(1024)(128)(4,1)} %bitcast.93), calls=%async_computation.8 | async-start | bytes 8388608
  117.8 19.1 %slice-start.3 = ((s8[14155776]{0:T(1024)(128)(4,1)}), s8[1572864]{0:T(1024)(128)(4,1)S(1)}, s32[]{:S(2)}) async-start(s8[14155776]{0:T(1024)(128)(4,1)} %bitcast.93), calls=%async_computation.9 | async-start | bytes 3145728
  136.9 77.8 %copy-start.1 = (bf16[1536,32]{0,1:T(8,128)(2,1)S(1)}, bf16[1536,32]{0,1:T(8,128)(2,1)}, u32[]{:S(2)}) copy-start(bf16[1536,32]{0,1:T(8,128)(2,1)} %param.20) | copy-start | bytes 294916
  140.0 8.0 %all-to-all-start.4 = ((bf16[4,8,1536]{2,1,0:T(8,128)(2,1)}), bf16[4,8,1536]{2,1,0:T(8,128)(2,1)S(1)}, u32[]{:S(2)}, u32[]{:S(2)}) async-start(bf16[4,8,1536]{2,1,0:T(8,128)(2,1)} %fusion.19), calls=%async_computation.4 | async-start | bytes 196608 | tf_op jit(solution)/shard_map/all_to_all | solution.py:112
  190.7 15.0 %all-to-all-start.5 = ((bf16[4,2,6144]{2,1,0:T(2,128)(2,1)}), bf16[4,2,6144]{2,1,0:T(2,128)(2,1)S(1)}, u32[]{:S(2)}, u32[]{:S(2)}) async-start(bf16[4,2,6144]{2,1,0:T(2,128)(2,1)} %reshape.134), calls=%async_computation.5 | async-start | bytes 196608 | tf_op jit(solution)/shard_map/all_to_all | solution.py:113
where the time goes:
time: 218 us; the launch traced here: 215 us
  other arithmetic  40.8 us (19%)
  local copies, waits for them, and re-layouts  39.9 us (18%)
  blocking collectives  39 us (18%)
  waiting for transfers between devices  35 us (16%)
  starting transfers between devices  32.5 us (15%)
  matrix products  27.1 us (12%)
    unnamed x2, other arithmetic  34.4 us
    all_to_all x1, waiting for transfers between devices, body(): lax.all_to_all(exclusive, 'seq', split_axis=0, concat_axis=0, tiled=True)  17.9 us
    slice x5, local copies, waits for them, and re-layouts, body(): lax.associative_scan(link_states, (element_decay, arrived_state), axis=0)[1]  15.9 us
    unnamed x35, local copies, waits for them, and re-layouts  13.7 us
    all_to_all x1, starting transfers between devices, body(): lax.all_to_all(returned[None], 'exp', split_axis=2, concat_axis=0, tiled=...  12.7 us
    all_gather x1, blocking collectives, body(): gathered = lax.all_gather(arrived, 'seq', axis=0, tiled=True)  11.6 us
    all_gather x1, blocking collectives, body(): lax.all_gather(hidden, 'seq', axis=1, tiled=True)  11.5 us
    all_to_all x1, waiting for transfers between devices, body(): lax.all_to_all(flat_state, 'seq', split_axis=0, concat_axis=0, tiled=True)  9.57 us
  transfers between devices with their start and end apart: 6, of which 5 were waited for; matrix products, arithmetic and copies ran while one was open for 8% of the time, Pallas kernels for 0%

commit v1 on v0

--- a/solution.py
+++ b/solution.py
@@ -1,6 +1,10 @@
+import functools
+
 import jax
 import jax.numpy as jnp
 from jax import lax
+from jax.experimental import pallas as pl
+from jax.experimental.pallas import tpu as pltpu
 from jax.sharding import PartitionSpec as P
 
 D = 6144
@@ -13,7 +17,7 @@
     return (earlier[0] * later[0], later[0] * earlier[1] + later[1])
 
 
-def body(
+def plain_body(
     residual,
     query_rows,
     key_rows,
@@ -118,6 +122,572 @@
     return (mixed_f + combined).astype(jnp.bfloat16)
 
 
+MESH = pl.DeviceIdType.MESH
+F32 = jnp.float32
+BF16 = jnp.bfloat16
+WEIGHT_CUTS = 4
+
+
+def layer_kernel(
+    ns,
+    nx,
+    group,
+    residual,
+    query,
+    key,
+    value,
+    log_decay,
+    attn_gain,
+    norm_gain,
+    router,
+    ids,
+    priority,
+    gate_hbm,
+    up_hbm,
+    down_hbm,
+    out,
+    weights_in,
+    weights_down,
+    padded,
+    cum_rows,
+    mixed,
+    chain_out,
+    chain_in,
+    sums_out,
+    sums_in,
+    slots_out,
+    slots_in,
+    inverse_out,
+    inverse_in,
+    total_in,
+    hidden_all,
+    total_out,
+    back_out,
+    back_in,
+    weight_sems,
+    chain_sems,
+    sums_send,
+    sums_recv,
+    slots_send,
+    slots_recv,
+    inverse_send,
+    inverse_recv,
+    hidden_send,
+    hidden_recv,
+    back_send,
+    back_recv,
+):
+    rows, width = residual.shape
+    heads = width // HEAD
+    half = width // 2
+    depth = weights_in.shape[0]
+    ff = gate_hbm.shape[2]
+    s = lax.axis_index("seq")
+    x = lax.axis_index("exp")
+
+    weight_copies = []
+    cut = depth // WEIGHT_CUTS
+    for i in range(WEIGHT_CUTS):
+        at = pl.ds(i * cut, cut)
+        weight_copies.append(
+            pltpu.make_async_copy(
+                gate_hbm.at[0, at, :], weights_in.at[at, pl.ds(0, ff)], weight_sems.at[0, i]
+            )
+        )
+        weight_copies.append(
+            pltpu.make_async_copy(
+                up_hbm.at[0, at, :], weights_in.at[at, pl.ds(ff, ff)], weight_sems.at[1, i]
+            )
+        )
+    down_copies = []
+    cut = weights_down.shape[0] // WEIGHT_CUTS
+    for i in range(WEIGHT_CUTS):
+        at = pl.ds(i * cut, cut)
+        down_copies.append(
+            pltpu.make_async_copy(down_hbm.at[0, at, :], weights_down.at[at, :], weight_sems.at[2, i])
+        )
+    for copy in weight_copies + down_copies:
+        copy.start()
+
+    barrier = pltpu.get_barrier_semaphore()
+    peers = [(a, b) for a in range(ns) for b in range(nx) if (a, b) != (0, 0)]
+
+    def peer(a, b):
+        return {"seq": lax.rem(s + a, ns), "exp": lax.rem(x + b, nx)}
+
+    for a, b in peers:
+        pl.semaphore_signal(barrier, inc=1, device_id=peer(a, b), device_id_type=MESH)
+
+    row_at = lax.broadcasted_iota(jnp.int32, (rows, rows), 0)
+    lane_at = lax.broadcasted_iota(jnp.int32, (rows, rows), 1)
+    id_cols = [ids[:, i : i + 1] for i in range(2)]
+    ids_t = jnp.where(
+        lane_at == 0,
+        id_cols[0].astype(F32),
+        jnp.where(lane_at == 1, id_cols[1].astype(F32), 0.0),
+    ).T
+    id_rows = [ids_t[i : i + 1, :] for i in range(2)]
+    order = jnp.broadcast_to(priority[...].astype(F32), (rows, rows))
+    earlier = jnp.where(order.T < order, 1.0, 0.0).astype(BF16)
+    expert_rows = -(-nx // 8) * 8
+    expert_at = lax.broadcasted_iota(jnp.int32, (expert_rows, rows), 0).astype(F32)
+    member = jnp.where((id_rows[0] == expert_at) | (id_rows[1] == expert_at), 1.0, 0.0)
+    rank = jnp.dot(member.astype(BF16), earlier, preferred_element_type=F32)
+    slot_at = lax.broadcasted_iota(jnp.int32, (CAP, rows), 0).astype(F32)
+    rank = jnp.where(member > 0.5, rank, -1.0)
+    place = [jnp.where(rank[e : e + 1, :] == slot_at, 1.0, 0.0) for e in range(nx)]
+    place_all = jnp.concatenate(place, axis=0)
+
+    padded[...] = jnp.zeros_like(padded)
+    padded[:, :heads] = log_decay[...]
+    lower = jnp.where(row_at >= lane_at, 1.0, 0.0).astype(F32)
+    cumulative = jnp.dot(
+        lower, padded[...], precision=lax.Precision.HIGHEST, preferred_element_type=F32
+    )
+    padded[...] = cumulative
+    cum_rows[...] = cumulative.T
+
+    @pl.when(s == 0)
+    def _():
+        chain_in[...] = jnp.zeros_like(chain_in)
+
+    pl.semaphore_wait(barrier, len(peers))
+
+    def chain_copy(i):
+        return pltpu.make_async_remote_copy(
+            src_ref=chain_out.at[i],
+            dst_ref=chain_in.at[i],
+            send_sem=chain_sems.at[0, i],
+            recv_sem=chain_sems.at[1, i],
+            device_id={"seq": lax.rem(s + 1, ns)},
+            device_id_type=MESH,
+        )
+
+    causal = row_at >= lane_at
+
+    def attend(i, carry):
+        held = []
+        for g in range(group):
+            head = i * group + g
+            at = pl.ds(pl.multiple_of(head * HEAD, HEAD), HEAD)
+            col = jnp.sum(jnp.where(lane_at == head, padded[...], 0.0), axis=1, keepdims=True)
+            row = cum_rows[pl.ds(head, 1), :]
+            last = col[rows - 1 : rows, :]
+            q, k, v = query[:, at], key[:, at], value[:, at]
+            keyed = (k.astype(F32) * jnp.exp(last - col)).astype(BF16)
+            state = lax.dot_general(
+                keyed, v, (((0,), (0,)), ((), ())), preferred_element_type=F32
+            )
+            scores = lax.dot_general(q, k, (((1,), (1,)), ((), ())), preferred_element_type=F32)
+            spread = jnp.where(causal, col - row, 0.0)
+            weights = jnp.where(causal, scores * jnp.exp(spread), 0.0).astype(BF16)
+            local = jnp.dot(weights, v, preferred_element_type=F32)
+            held.append((at, q, state, jnp.exp(last), local, jnp.exp(col)))
+
+        @pl.when(s > 0)
+        def _():
+            chain_copy(i).wait_recv()
+
+        @pl.when(s < ns - 1)
+        def _():
+            for g in range(group):
+                prior = chain_in[i, g].astype(F32)
+                chain_out[i, g] = (held[g][3] * prior + held[g][2]).astype(BF16)
+            chain_copy(i).start()
+
+        for g in range(group):
+            at, q, _, _, local, grown = held[g]
+            inter = jnp.dot(q, chain_in[i, g], preferred_element_type=F32)
+            attended = local + grown * inter
+            mean = jnp.sum(attended * attended, axis=1, keepdims=True) / HEAD
+            normed = attended * lax.rsqrt(mean + 1e-06) * attn_gain[:, at]
+            mixed[:, at] = (residual[:, at].astype(F32) + normed).astype(BF16)
+        return carry
+
+    lax.fori_loop(0, heads // group, attend, 0)
+
+    mixed_f = mixed[...].astype(F32)
+    gained = mixed_f * norm_gain[...]
+    tokens = gained.astype(BF16)
+    place_b = place_all.astype(BF16)
+    for h in range(2):
+        part = jnp.dot(
+            place_b, tokens[:, h * half : (h + 1) * half], preferred_element_type=F32
+        )
+        if h == 0:
+            first = part
+    for e in range(nx):
+        at = slice(e * CAP, (e + 1) * CAP)
+        slots_out[e] = jnp.concatenate([first[at], part[at]], axis=0).astype(BF16)
+    slots_in[s, x] = slots_out[x]
+
+    def slots_copy(a, b):
+        return pltpu.make_async_remote_copy(
+            src_ref=slots_out.at[lax.rem(x + b, nx)],
+            dst_ref=slots_in.at[s, x],
+            send_sem=slots_send.at[a, b],
+            recv_sem=slots_recv.at[s, x],
+            device_id=peer(a, b),
+            device_id_type=MESH,
+        )
+
+    def slots_arrive(block, source):
+        return pltpu.make_async_remote_copy(
+            src_ref=slots_out.at[0],
+            dst_ref=slots_in.at[block, source],
+            send_sem=slots_send.at[0, 0],
+            recv_sem=slots_recv.at[block, source],
+            device_id=peer(1, 1),
+            device_id_type=MESH,
+        )
+
+    for a, b in peers:
+        slots_copy(a, b).start()
+
+    rest = (gained - tokens.astype(F32)).astype(BF16)
+    logits = jnp.dot(tokens, router[...], preferred_element_type=F32) + jnp.dot(
+        rest, router[...], preferred_element_type=F32
+    )
+    expert_lane = lax.broadcasted_iota(jnp.int32, logits.shape, 1)
+    picked = [
+        jnp.sum(jnp.where(expert_lane == c, logits, 0.0), axis=1, keepdims=True) for c in id_cols
+    ]
+    squares = jnp.sum(mixed_f * mixed_f, axis=1, keepdims=True)
+    sums = jnp.where(
+        lane_at == 0,
+        picked[0],
+        jnp.where(lane_at == 1, picked[1], jnp.where(lane_at == 2, squares, 0.0)),
+    ).T
+    sums_out[...] = sums[0:8, :]
+    sums_in[x] = sums[0:8, :]
+
+    def sums_copy(b):
+        return pltpu.make_async_remote_copy(
+            src_ref=sums_out,
+            dst_ref=sums_in.at[x],
+            send_sem=sums_send.at[b],
+            recv_sem=sums_recv.at[x],
+            device_id=peer(0, b),
+            device_id_type=MESH,
+        )
+
+    def sums_arrive(b):
+        source = lax.rem(x + b, nx)
+        return pltpu.make_async_remote_copy(
+            src_ref=sums_out,
+            dst_ref=sums_in.at[source],
+            send_sem=sums_send.at[b],
+            recv_sem=sums_recv.at[source],
+            device_id=peer(0, b),
+            device_id_type=MESH,
+        )
+
+    for b in range(1, nx):
+        sums_copy(b).start()
+    for b in range(1, nx):
+        sums_arrive(b).wait_recv()
+    added = sums_in[0]
+    for b in range(1, nx):
+        added = added + sums_in[b]
+    inverse = lax.rsqrt(added[2:3, :] / (width * nx) + 1e-06)
+    probs = [jax.nn.sigmoid(added[i : i + 1, :] * inverse) for i in range(2)]
+    gates = [p / (probs[0] + probs[1]) for p in probs]
+    slot_inverse = jnp.sum(place_all * inverse, axis=1, keepdims=True)
+    slot_inverse = jnp.broadcast_to(slot_inverse, place_all.shape)
+    for e in range(nx):
+        inverse_out[e] = slot_inverse[e * CAP : (e + 1) * CAP, :]
+    inverse_in[s] = inverse_out[x]
+
+    def inverse_copy(a):
+        return pltpu.make_async_remote_copy(
+            src_ref=inverse_out.at[x],
+            dst_ref=inverse_in.at[s],
+            send_sem=inverse_send.at[a],
+            recv_sem=inverse_recv.at[s],
+            device_id=peer(a, 0),
+            device_id_type=MESH,
+        )
+
+    def inverse_arrive(a):
+        source = lax.rem(s + a, ns)
+        return pltpu.make_async_remote_copy(
+            src_ref=inverse_out.at[x],
+            dst_ref=inverse_in.at[source],
+            send_sem=inverse_send.at[a],
+            recv_sem=inverse_recv.at[source],
+            device_id=peer(a, 0),
+            device_id_type=MESH,
+        )
+
+    for a in range(1, ns):
+        inverse_copy(a).start()
+
+    weighted = jnp.concatenate(
+        [
+            place[e]
+            * (
+                jnp.where(id_rows[0] == e, gates[0], 0.0)
+                + jnp.where(id_rows[1] == e, gates[1], 0.0)
+            )
+            for e in range(nx)
+        ],
+        axis=0,
+    )
+    slots = nx * CAP
+    padded[...] = jnp.zeros_like(padded)
+    padded[:slots, :] = weighted
+    weighted = padded[...].T[:, :slots]
+    weighted_high = weighted.astype(BF16)
+    weighted_low = (weighted - weighted_high.astype(F32)).astype(BF16)
+
+    for copy in weight_copies:
+        copy.wait()
+    for b in range(nx):
+        source = lax.rem(x + b, nx)
+        for a in range(ns):
+            if (a, b) != (0, 0):
+                slots_arrive(lax.rem(s + a, ns), source).wait_recv()
+        arrived = [slots_in[i, source].astype(F32) for i in range(ns)]
+        for h in range(2):
+            chunk = jnp.concatenate([p[h * CAP : (h + 1) * CAP] for p in arrived], axis=0)
+            start = pl.multiple_of(source * width + h * half, half)
+            product = jnp.dot(
+                chunk.astype(BF16), weights_in[pl.ds(start, half), :], preferred_element_type=F32
+            )
+            if b == 0 and h == 0:
+                total_in[...] = product
+            else:
+                total_in[...] += product
+    for a in range(1, ns):
+        inverse_arrive(a).wait_recv()
+    scale = jnp.concatenate([inverse_in[i] for i in range(ns)], axis=0)[:, :1]
+    gate = total_in[:, :ff] * scale
+    up = total_in[:, ff:] * scale
+    hidden_all[s] = (jax.nn.silu(gate) * up).astype(BF16)
+
+    def hidden_copy(a):
+        return pltpu.make_async_remote_copy(
+            src_ref=hidden_all.at[s],
+            dst_ref=hidden_all.at[s],
+            send_sem=hidden_send.at[a],
+            recv_sem=hidden_recv.at[s],
+            device_id=peer(a, 0),
+            device_id_type=MESH,
+        )
+
+    def hidden_arrive(a):
+        source = lax.rem(s + a, ns)
+        return pltpu.make_async_remote_copy(
+            src_ref=hidden_all.at[s],
+            dst_ref=hidden_all.at[source],
+            send_sem=hidden_send.at[a],
+            recv_sem=hidden_recv.at[source],
+            device_id=peer(a, 0),
+            device_id_type=MESH,
+        )
+
+    for a in range(1, ns):
+        hidden_copy(a).start()
+    for copy in down_copies:
+        copy.wait()
+    for a in range(ns):
+        source = lax.rem(s + a, ns)
+        if a:
+            hidden_arrive(a).wait_recv()
+        start = pl.multiple_of(source * ff, HEAD)
+        product = jnp.dot(
+            hidden_all[source], weights_down[pl.ds(start, ff), :], preferred_element_type=F32
+        )
+        if a == 0:
+            total_out[...] = product
+        else:
+            total_out[...] += product
+
+    for b in range(ns):
+        at = slice(b * CAP, (b + 1) * CAP)
+        back_out[b] = jnp.concatenate(
+            [total_out[at, :half], total_out[at, half:]], axis=0
+        ).astype(BF16)
+
+    def back_copy(block):
+        return pltpu.make_async_remote_copy(
+            src_ref=back_out.at[block],
+            dst_ref=back_in.at[x],
+            send_sem=back_send.at[block],
+            recv_sem=back_recv.at[x],
+            device_id={"seq": block, "exp": s},
+            device_id_type=MESH,
+        )
+
+    def back_arrive(e):
+        return pltpu.make_async_remote_copy(
+            src_ref=back_out.at[0],
+            dst_ref=back_in.at[e],
+            send_sem=back_send.at[0],
+            recv_sem=back_recv.at[e],
+            device_id={"seq": x, "exp": e},
+            device_id_type=MESH,
+        )
+
+    for a in range(ns):
+        block = lax.rem(s + a, ns)
+        if a:
+            back_copy(block).start()
+        else:
+
+            @pl.when(x != s)
+            def _():
+                back_copy(block).start()
+
+            @pl.when(x == s)
+            def _():
+                back_in[x] = back_out[block]
+
+    for b in range(nx):
+        e = lax.rem(x + b, nx)
+        if b:
+            back_arrive(e).wait_recv()
+        else:
+
+            @pl.when(x != s)
+            def _():
+                back_arrive(e).wait_recv()
+
+    returned = [back_in[e].astype(F32) for e in range(nx)]
+    for h in range(2):
+        expert_out = jnp.concatenate(
+            [r[h * CAP : (h + 1) * CAP] for r in returned], axis=0
+        ).astype(BF16)
+        combined = jnp.dot(weighted_high, expert_out, preferred_element_type=F32) + jnp.dot(
+            weighted_low, expert_out, preferred_element_type=F32
+        )
+        at = slice(h * half, (h + 1) * half)
+        out[:, at] = (mixed[:, at].astype(F32) + combined).astype(BF16)
+
+    @pl.when(s < ns - 1)
+    def _():
+        for i in range(heads // group):
+            chain_copy(i).wait_send()
+
+    for a, b in peers:
+        slots_copy(a, b).wait_send()
+    for b in range(1, nx):
+        sums_copy(b).wait_send()
+    for a in range(1, ns):
+        inverse_copy(a).wait_send()
+        hidden_copy(a).wait_send()
+    for a in range(ns):
+        block = lax.rem(s + a, ns)
+        if a:
+            back_copy(block).wait_send()
+        else:
+
+            @pl.when(x != s)
+            def _():
+                back_copy(block).wait_send()
+
+
+def fused_body(
+    residual,
+    query_rows,
+    key_rows,
+    value_rows,
+    log_decay,
+    attn_gain,
+    norm_gain,
+    router,
+    expert_ids,
+    priority,
+    gate_weight,
+    up_weight,
+    down_weight,
+):
+    ns, nx = lax.axis_size("seq"), lax.axis_size("exp")
+    rows, width = residual.shape
+    heads = width // HEAD
+    group = 2 if heads % 2 == 0 else 1
+    steps = heads // group
+    depth, ff = gate_weight.shape[1:]
+    half = width // 2
+    dma = pltpu.SemaphoreType.DMA
+    in_vmem = pl.BlockSpec(memory_space=pltpu.VMEM)
+    in_place = pl.BlockSpec(memory_space=pl.ANY)
+    return pl.pallas_call(
+        functools.partial(layer_kernel, ns, nx, group),
+        out_shape=jax.ShapeDtypeStruct((rows, width), BF16),
+        in_specs=[in_vmem] * 10 + [in_place] * 3,
+        out_specs=in_vmem,
+        scratch_shapes=[
+            pltpu.VMEM((depth, 2 * ff), BF16),
+            pltpu.VMEM(down_weight.shape[1:], BF16),
+            pltpu.VMEM((rows, rows), F32),
+            pltpu.VMEM((rows, rows), F32),
+            pltpu.VMEM((rows, width), BF16),
+            pltpu.VMEM((steps, group, HEAD, HEAD), BF16),
+            pltpu.VMEM((steps, group, HEAD, HEAD), BF16),
+            pltpu.VMEM((8, rows), F32),
+            pltpu.VMEM((nx, 8, rows), F32),
+            pltpu.VMEM((nx, 2 * CAP, half), BF16),
+            pltpu.VMEM((ns, nx, 2 * CAP, half), BF16),
+            pltpu.VMEM((nx, CAP, rows), F32),
+            pltpu.VMEM((ns, CAP, rows), F32),
+            pltpu.VMEM((ns * CAP, 2 * ff), F32),
+            pltpu.VMEM((ns, ns * CAP, ff), BF16),
+            pltpu.VMEM((ns * CAP, width), F32),
+            pltpu.VMEM((ns, 2 * CAP, half), BF16),
+            pltpu.VMEM((nx, 2 * CAP, half), BF16),
+            dma((3, WEIGHT_CUTS)),
+            dma((2, steps)),
+            dma((nx,)),
+            dma((nx,)),
+            dma((ns, nx)),
+            dma((ns, nx)),
+            dma((ns,)),
+            dma((ns,)),
+            dma((ns,)),
+            dma((ns,)),
+            dma((ns,)),
+            dma((nx,)),
+        ],
+        compiler_params=pltpu.CompilerParams(
+            collective_id=0, has_side_effects=True, vmem_limit_bytes=60 * 1024 * 1024
+        ),
+        cost_estimate=pl.CostEstimate(
+            flops=6 * ns * CAP * depth * ff,
+            bytes_accessed=6 * depth * ff,
+            transcendentals=heads * rows * rows,
+        ),
+    )(
+        residual,
+        query_rows,
+        key_rows,
+        value_rows,
+        log_decay,
+        attn_gain.reshape(1, width),
+        norm_gain.reshape(1, width),
+        router,
+        expert_ids,
+        priority,
+        gate_weight,
+        up_weight,
+        down_weight,
+    )
+
+
+def body(*args):
+    rows, width = args[0].shape
+    ff, columns = args[10].shape[2], args[12].shape[2]
+    aligned = (
+        rows == HEAD
+        and ff % HEAD == 0
+        and width % (2 * HEAD) == 0
+        and columns == width
+        and args[10].shape[0] == 1
+        and lax.axis_size("seq") == lax.axis_size("exp")
+    )
+    return (fused_body if aligned else plain_body)(*args)
+
+
 def solution(mesh):
     return jax.shard_map(
         body,

time: 218 us -> 68.8 us (0.32)
  the two profiles are of different devices: /device:TPU:3 before, /device:TPU:1 now
where the time goes in v1:
time: 68.8 us; the launch traced here: 68.5 us
  Pallas kernels  59.5 us (86%)
  local copies, waits for them, and re-layouts  8.98 us (13%)
    pallas_call x1, Pallas kernels, fused_body(): pl.pallas_call(functools.partial(layer_kernel, ns, nx, group), out_shape=...  59.5 us
    unnamed x4, local copies, waits for them, and re-layouts  6.4 us

profile of v1, /device:TPU:1, one launch (start us, length us, event | category | flops | bytes accessed | tf_op | source)
XLA Modules:
  0.0 68.5 jit_solution(16769357635131263335)
XLA Ops:
  0.0 1.3 %reshape.6.attn_gain = f32[1,1536]{1,0:T(1,128)} reshape(f32[1536]{0:T(1024)} %param.18) | data formatting | bytes 12288 | tf_op jit(solution)/shard_map/reshape | solution.py:666
  1.3 1.3 %reshape.7.norm_gain = f32[1,1536]{1,0:T(1,128)} reshape(f32[1536]{0:T(1024)} %param.19) | data formatting | bytes 12288 | tf_op jit(solution)/shard_map/reshape | solution.py:667
  2.6 1.4 %copy.14.log_decay = f32[128,12]{1,0:T(8,128)} copy(f32[128,12]{0,1:T(8,128)} %param.17) | data formatting | bytes 12288 | tf_op args[4]
  4.0 1.4 %copy.16.ids = s32[128,2]{1,0:T(8,128)} copy(s32[128,2]{0,1:T(2,128)} %param.21) | data formatting | bytes 2048 | tf_op args[8]
  5.4 1.8 %copy.15.router = bf16[1536,32]{1,0:T(8,128)(2,1)} copy(bf16[1536,32]{0,1:T(8,128)(2,1)} %param.20) | data formatting | bytes 196608 | tf_op args[7]
  7.2 59.5 %shard_map.127 = bf16[128,1536]{1,0:T(8,128)(2,1)} custom-call(bf16[128,1536]{1,0:T(8,128)(2,1)} %residual.1, bf16[128,1536]{1,0:T(8,128)(2,1)} %query.1, bf16[128,1536]{1,0:T(8,128)(2,1)} %key.1, bf16[128,1536]{1,0:T(8,128)(2,1)} %value.1, f32[128,12]{1,0:T(8,128)} %copy.14.log_decay, f32[1,1536]{1,0:T(1,128)} %reshape.6.attn_gain, ...), custom_call_target="tpu_custom_call" | custom-call | flops 1358954496 | bytes 42467328 | tf_op jit(solution)/shard_map/pallas_call | solution.py:615
  66.7 1.8 %copy.18 = bf16[128,1536]{1,0:T(8,128)(2,1)} copy(bf16[128,1536]{1,0:T(8,128)(2,1)} %shard_map.127) | data formatting | bytes 786432
